TPU v7x, 32 devices: a whole 2x2x4 slice. The times are simulated.
32 devices in a mesh: groups: 1, patch: 16 (over z, y, x), image: 2 (over core).
Axes of the slice: x: 2, y: 2, z: 4, core: 2. Of those that a mesh axis runs over, the one named last changes fastest.
Arguments:
- queries: bfloat16 [2, 128, 1280], P(('groups', 'image'), 'patch'), may hold values from -12 to 12
- fresh_keys: bfloat16 [2, 128, 1280], P(('groups', 'image'), 'patch'), may hold values from -4 to 4
- fresh_values: bfloat16 [2, 128, 1280], P(('groups', 'image'), 'patch'), may hold values from -4 to 4
- stale_keys: bfloat16 [2, 128, 1280], P(('groups', 'image'), 'patch'), may hold values from -12 to 12
- stale_values: bfloat16 [2, 128, 1280], P(('groups', 'image'), 'patch'), may hold values from -4 to 4
- residual: bfloat16 [2, 128, 2560], P(('groups', 'image'), 'patch'), may hold values from -6 to 6
- out_proj: bfloat16 [1280, 2560], P('image'), may hold values from -0.15625 to 0.15625
- norm_gain: float32 [2560], replicated, may hold values from 0.25 to 1.75
- router: float32 [2560, 4], replicated, may hold values from -0.125 to 0.125
- expert_ids: int32 [2, 128, 2], P(('groups', 'image'), 'patch'), may hold values from 0 to 3, all different within a row; in each aligned block of 8 rows (0 to 7, 8 to 15, ..., all dimensions but the last counted through in order) at most 8 rows name the same one
- routed_gate: bfloat16 [16, 384, 2560], P('patch', 'image'), may hold values from -0.125 to 0.125
- routed_up: bfloat16 [16, 384, 2560], P('patch', 'image'), may hold values from -0.125 to 0.125
- routed_down: bfloat16 [16, 384, 2560], P('patch', 'image'), may hold values from -0.15625 to 0.15625
- shared_gate: bfloat16 [768, 2560], P('image'), may hold values from -0.125 to 0.125
- shared_up: bfloat16 [768, 2560], P('image'), may hold values from -0.125 to 0.125
- shared_down: bfloat16 [768, 2560], P('image'), may hold values from -0.21875 to 0.21875
Outputs:
- attended: bfloat16 [2, 128, 2560], P(('groups', 'image'), 'patch')
- block_out: bfloat16 [2, 128, 2560], P(('groups', 'image'), 'patch')
Inputs may be any that keep to these rules, and one draw needn't show every extreme that they name: `expert_ids`: each token names two different experts and every expert is named by some token. Among the 8 tokens of one device (aligned blocks of rows, images before positions) no expert is named more than 8 times, a bound that some block reaches.
All inputs are finite; a program needn't handle non-finite values.
Results may differ from a plain program's by a relative error of at most 0.017.
Values may be sent and summed in bfloat16 or wider, within the bound.
A program may use at most 64 MiB of HBM per device.

v0:
```python
import jax
import jax.numpy as jnp
from jax import lax
from jax.sharding import PartitionSpec as P

HD = 128


EPS = 1e-06


def project_rows(in_rows, weight_rows):
    return lax.dot_general(
        in_rows, weight_rows, (((1,), (1,)), ((), ())), preferred_element_type=jnp.float32
    )


def swiglu_rows(in_rows, gate_rows, up_rows):
    gate_vals = project_rows(in_rows, gate_rows)
    up_vals = project_rows(in_rows, up_rows)
    return (jax.nn.silu(gate_vals) * up_vals).astype(jnp.bfloat16)


def expert_part(buffer, gate_rows, up_rows, down_rows):
    buffer_shape = buffer.shape
    hidden = swiglu_rows(buffer.reshape(-1, buffer_shape[-1]), gate_rows, up_rows)
    partial_value = jnp.dot(hidden, down_rows, preferred_element_type=jnp.float32)
    return partial_value.astype(jnp.bfloat16).reshape(buffer_shape)


def per_device(
    queries,
    fresh_keys,
    fresh_values,
    stale_keys,
    stale_values,
    residual,
    out_proj,
    norm_gain,
    router,
    expert_ids,
    routed_gate,
    routed_up,
    routed_down,
    shared_gate,
    shared_up,
    shared_down,
):
    patch_rows = queries.shape[1]
    head_width = queries.shape[2]
    num_heads = head_width // HD
    model_width = residual.shape[2]
    factor = HD ** (-0.5)
    own_query = queries[0].reshape(patch_rows, num_heads, HD)
    own_keys = fresh_keys[0].reshape(patch_rows, num_heads, HD)
    own_values = fresh_values[0].reshape(patch_rows, num_heads, HD)
    first_scores = (
        jnp.einsum("qhd,khd->hqk", own_query, own_keys, preferred_element_type=jnp.float32) * factor
    )
    first_max = jnp.max(first_scores, axis=-1)
    first_exp = jnp.exp(first_scores - first_max[..., None])
    first_sum = jnp.sum(first_exp, axis=-1)
    first_acc = jnp.einsum(
        "hqk,khd->hqd",
        first_exp.astype(jnp.bfloat16),
        own_values,
        preferred_element_type=jnp.float32,
    )
    own_start = lax.axis_index("patch") * patch_rows
    pieces = (
        lax.all_gather(stale_keys[0], "patch", axis=0, tiled=True),
        lax.all_gather(stale_values[0], "patch", axis=0, tiled=True),
    )
    key_count = pieces[0].shape[0]
    piece_keys = pieces[0].reshape(key_count, num_heads, HD)
    piece_values = pieces[1].reshape(key_count, num_heads, HD)
    positions = jnp.arange(key_count, dtype=jnp.int32)
    is_own = (positions >= own_start) & (positions < own_start + patch_rows)
    scores = (
        jnp.einsum("qhd,khd->hqk", own_query, piece_keys, preferred_element_type=jnp.float32)
        * factor
    )
    scores = jnp.where(is_own[None, None, :], -1e30, scores)
    new_max = jnp.maximum(first_max, jnp.max(scores, axis=-1))
    exp_scores = jnp.exp(scores - new_max[..., None])
    rescale = jnp.exp(first_max - new_max)
    new_acc = first_acc * rescale[..., None] + jnp.einsum(
        "hqk,khd->hqd",
        exp_scores.astype(jnp.bfloat16),
        piece_values,
        preferred_element_type=jnp.float32,
    )
    fin_sum = first_sum * rescale + jnp.sum(exp_scores, axis=-1)
    attn_rows = (
        jnp.transpose(new_acc / fin_sum[..., None], (1, 0, 2))
        .reshape(patch_rows, head_width)
        .astype(jnp.bfloat16)
    )
    heads_split = lax.all_to_all(attn_rows, "image", split_axis=1, concat_axis=0, tiled=True)
    block_rows = heads_split
    projected = lax.psum_scatter(
        jnp.dot(block_rows, out_proj, preferred_element_type=jnp.float32).astype(jnp.bfloat16),
        "image",
        scatter_dimension=0,
        tiled=True,
    ).astype(jnp.float32)
    attended = (residual[0].astype(jnp.float32) + projected).astype(jnp.bfloat16)
    mid_f32 = attended.astype(jnp.float32)
    mean_sq = jnp.mean(mid_f32 * mid_f32, axis=-1, keepdims=True)
    normed = (mid_f32 * lax.rsqrt(mean_sq + EPS) * norm_gain).astype(jnp.bfloat16)
    shared_rows = lax.all_gather(normed, "image", axis=0, tiled=True)
    block_rows = shared_rows
    shared_out = lax.psum_scatter(
        jnp.dot(
            swiglu_rows(block_rows, shared_gate, shared_up),
            shared_down,
            preferred_element_type=jnp.float32,
        ).astype(jnp.bfloat16),
        "image",
        scatter_dimension=0,
        tiled=True,
    ).astype(jnp.float32)
    logits = jnp.dot(normed.astype(jnp.float32), router, precision=lax.Precision.HIGHEST)
    gate_probs = jax.nn.sigmoid(logits)
    num_experts = router.shape[1]
    capacity = max(2, min(patch_rows, 4 * patch_rows // num_experts))
    ids_flat = expert_ids[0].reshape(-1)
    onehot = ids_flat[:, None] == jnp.arange(num_experts, dtype=jnp.int32)[None, :]
    pair_weight = jnp.sum(jnp.where(onehot, jnp.repeat(gate_probs, 2, axis=0), 0.0), axis=1)
    onehot_count = onehot.astype(jnp.int32)
    earlier = jnp.cumsum(onehot_count, axis=0) - onehot_count
    slot_of = jnp.sum(earlier * onehot_count, axis=1)
    slot_index = ids_flat * capacity + slot_of
    selector = (
        jnp.arange(num_experts * capacity, dtype=jnp.int32)[:, None] == slot_index[None, :]
    ).astype(jnp.bfloat16)
    pair_rows = jnp.repeat(normed, 2, axis=0)
    buffer = jnp.dot(selector, pair_rows, preferred_element_type=jnp.float32).astype(jnp.bfloat16)
    buffer = buffer.reshape(num_experts, capacity, model_width)
    patch_count = lax.axis_size("patch")
    image_count = lax.axis_size("image")
    per_expert = patch_count * image_count // num_experts
    send_rows = jnp.repeat(buffer, per_expert, axis=0)
    partial_value = expert_part(
        lax.all_to_all(send_rows, ("patch", "image"), split_axis=0, concat_axis=0, tiled=True),
        routed_gate[0],
        routed_up[0],
        routed_down[0],
    )
    returned = lax.all_to_all(
        partial_value, ("patch", "image"), split_axis=0, concat_axis=0, tiled=True
    )
    expert_out = jnp.sum(
        returned.reshape(num_experts, per_expert, capacity, model_width).astype(jnp.float32), axis=1
    )
    flat_out = expert_out.reshape(num_experts * capacity, model_width)
    pair_out = jnp.take(flat_out, slot_index, axis=0)
    routed = jnp.sum((pair_weight[:, None] * pair_out).reshape(patch_rows, 2, model_width), axis=1)
    block_out = (mid_f32 + shared_out + routed).astype(jnp.bfloat16)
    return (attended[None], block_out[None])


def solution(mesh):
    in_specs = (
        P(("groups", "image"), "patch", None),
        P(("groups", "image"), "patch", None),
        P(("groups", "image"), "patch", None),
        P(("groups", "image"), "patch", None),
        P(("groups", "image"), "patch", None),
        P(("groups", "image"), "patch", None),
        P("image", None),
        P(),
        P(),
        P(("groups", "image"), "patch", None),
        P("patch", "image", None),
        P("patch", "image", None),
        P("patch", "image", None),
        P("image", None),
        P("image", None),
        P("image", None),
    )
    out_specs = (P(("groups", "image"), "patch", None), P(("groups", "image"), "patch", None))
    return jax.shard_map(
        per_device, mesh=mesh, in_specs=in_specs, out_specs=out_specs, check_vma=False
    )
```

profile of v0, /device:TPU:0, one launch (start us, length us, event | category | flops | bytes accessed | tf_op | source)
XLA Modules:
  0.0 209.0 jit_solution(16156204992557187567)
XLA Ops:
  7.2 0.0 copy-start
  7.2 0.0 copy-start.11
  7.2 0.0 reduce-scatter.3.cloned.1.call-start
  7.3 47.0 %all-gather = bf16[1,128,1280]{2,1,0:T(8,128)(2,1)} all-gather(bf16[1,8,1280]{2,1,0:T(8,128)(2,1)} %param.19), channel_id=2, replica_groups=mesh['groups'=1,'patch'=16,'image'=2] {'patch'}, dimensions={1}, use_global_device_ids=true | all-gather | bytes 348160 | tf_op jit(solution)/shard_map/all_gather | solution.py:71
  54.2 1.9 copy.52
  56.1 0.9 fusion.68
  57.0 1.3 fusion.69
  58.3 39.8 %all-gather.1 = bf16[1,128,1280]{2,1,0:T(8,128)(2,1)} all-gather(bf16[1,8,1280]{2,1,0:T(8,128)(2,1)} %param.20), channel_id=3, replica_groups=mesh['groups'=1,'patch'=16,'image'=2] {'patch'}, dimensions={1}, use_global_device_ids=true | all-gather | bytes 348160 | tf_op jit(solution)/shard_map/all_gather | solution.py:72
  98.1 1.9 copy.54
  99.9 0.2 fusion.43
  100.1 1.3 convolution_bitcast_fusion
  101.4 0.0 copy-start.6
  101.4 0.0 copy-start.5
  101.4 0.0 copy-done.11
  101.4 0.0 copy-start.8
  101.4 0.2 fusion.16
  101.6 3.7 %all_to_all.26 = bf16[8,2,640]{2,0,1:T(8,128)(2,1)S(1)} all-to-all(bf16[8,2,640]{2,0,1:T(8,128)(2,1)S(1)} %bitcast.111), channel_id=1, replica_groups=mesh['groups'=1,'patch'=16,'image'=2] {'image'}, dimensions={1} | all-to-all | bytes 40960 | tf_op jit(solution)/shard_map/all_to_all | solution.py:99
  105.4 0.0 copy-done
  105.4 1.2 convolution_convert_fusion.3
  106.5 0.0 reduce-scatter.3.cloned.1.call-update
  106.6 0.0 copy-done.6
  106.6 0.1 copy.59
  106.7 0.1 reshape_squeeze.15
  106.7 0.1 fusion.62
  106.8 0.2 select_reduce_fusion
  107.0 0.0 copy-start.9
  107.1 5.2 %reduce-scatter.3.cloned.1.call-done = bf16[8,2560]{1,0:T(8,128)(2,1)} async-done(((bf16[16,2560]{1,0:T(8,128)(2,1)}), bf16[8,2560]{1,0:T(8,128)(2,1)}) %reduce-scatter.3.cloned.1.call-update) | async-done | bytes 40976 | tf_op jit(solution)/shard_map/reduce_scatter | solution.py:101
  112.2 0.0 copy-done.5
  112.2 0.9 fusion.34
  113.2 0.0 copy-done.9
  113.2 0.0 copy-done.8
  113.2 0.1 fusion.36
  113.3 0.2 fusion.1
  113.5 0.0 copy-start.2
  113.5 0.1 broadcast_in_dim.59
  113.6 38.8 %all_to_all.27 = bf16[32,8,2560]{2,1,0:T(8,128)(2,1)S(1)} all-to-all(bf16[32,8,2560]{2,1,0:T(8,128)(2,1)S(1)} %bitcast.107), channel_id=1, replica_groups=mesh['groups'=1,'patch'=16,'image'=2] {'patch','image'}, dimensions={0} | all-to-all | bytes 2621440 | tf_op jit(solution)/shard_map/all_to_all | solution.py:145
  152.4 1.1 copy-done.1
  153.5 0.0 copy-done.2
  153.5 0.6 fusion.4
  154.0 4.7 %fusion = bf16[32,8,2560]{2,1,0:T(8,128)(2,1)} fusion(bf16[1,192,2560]{2,1,0:T(8,128)(2,1)} %param.28, bf16[32,8,2560]{2,1,0:T(8,128)(2,1)} %copy-done.1, bf16[1,192,2560]{2,1,0:T(8,128)(2,1)} %param.27, f32[256,192]{0,1:T(8,128)S(1)} %fusion.4), kind=kOutput, calls=%fused_computation.2 | convolution fusion | flops 504266752 | bytes 4784128 | tf_op jit(solution)/shard_map/dot_general | solution.py:27
  158.7 3.5 %all-to-all-start.2 = ((bf16[32,8,2560]{2,1,0:T(8,128)(2,1)}), bf16[32,8,2560]{2,1,0:T(8,128)(2,1)}, u32[]{:S(2)}, u32[]{:S(2)}) async-start(bf16[32,8,2560]{2,1,0:T(8,128)(2,1)} %fusion), calls=%async_computation.4 | async-start | bytes 2621440 | tf_op jit(solution)/shard_map/all_to_all | solution.py:150
  162.3 0.0 reduce-scatter.5.cloned.1.call-start
  162.3 0.0 copy-done.10
  162.3 0.1 reduce_sum.78
  162.4 0.0 copy-done.7
  162.4 0.1 copy.62
  162.5 0.1 mul.123
  162.6 0.1 copy.60
  162.7 0.1 copy.61
  162.8 0.0 copy-done.4
  162.8 0.1 fusion.20
  162.9 0.1 select_reduce_fusion.1
  163.0 0.1 copy.58
  163.1 1.9 all_gather.11
  165.0 2.2 %fusion.70 = f32[16,384]{1,0:T(8,128)S(1)} fusion(bf16[16,2560]{1,0:T(8,128)(2,1)S(1)} %all_gather.11, bf16[384,2560]{1,0:T(8,128)(2,1)} %param.29), kind=kOutput, calls=%fused_computation.94 | convolution fusion | flops 31457280 | bytes 2072576 | tf_op jit(solution)/shard_map/dot_general | solution.py:13
  167.1 4.1 %convolution_convert_fusion.2 = bf16[16,2560]{1,0:T(8,128)(2,1)} fusion(bf16[384,2560]{1,0:T(8,128)(2,1)} %param.31, bf16[16,2560]{1,0:T(8,128)(2,1)S(1)} %all_gather.11, bf16[384,2560]{1,0:T(8,128)(2,1)} %param.30, f32[16,384]{1,0:T(8,128)S(1)} %fusion.70), kind=kOutput, calls=%fused_computation.5 | convolution fusion | flops 62992384 | bytes 4120576 | tf_op jit(solution)/shard_map/dot_general | solution.py:114
  171.2 0.0 reduce-scatter.5.cloned.1.call-update
  171.3 22.9 %all-to-all-done.2 = bf16[32,8,2560]{2,1,0:T(8,128)(2,1)} async-done(((bf16[32,8,2560]{2,1,0:T(8,128)(2,1)}), bf16[32,8,2560]{2,1,0:T(8,128)(2,1)}, u32[]{:S(2)}, u32[]{:S(2)}) %all-to-all-start.2) | async-done | bytes 1310752 | tf_op jit(solution)/shard_map/all_to_all | solution.py:150
  194.1 2.3 %convert_reduce_fusion = f32[4,8,2560]{2,1,0:T(8,128)} fusion(bf16[32,8,2560]{2,1,0:T(8,128)(2,1)} %all-to-all-done.2), kind=kLoop, calls=%fused_computation.7 | loop fusion | flops 1228800 | bytes 1638400 | tf_op jit(solution)/shard_map/reduce_sum | solution.py:153
  196.4 2.3 %gather_fusion = f32[16,2560]{1,0:T(8,128)} fusion(f32[32,2560]{1,0:T(8,128)} %bitcast.106, s32[1024]{0:T(1024)S(1)} %pad_clamp_fusion), kind=kCustom, calls=%fused_computation | custom fusion | bytes 327744 | tf_op jit(solution)/shard_map/jit(_take)/gather | solution.py:157
  198.7 1.0 gather.7
  199.7 0.9 multiply_reduce_fusion
  200.6 0.0 copy-done.3
  200.6 1.5 fusion.40
  (19 shorter events, 0.2 us)
Async XLA Ops:
  7.2 98.2 %copy-start = (bf16[640,2560]{1,0:T(8,128)(2,1)S(1)}, bf16[640,2560]{1,0:T(8,128)(2,1)}, u32[]{:S(2)}) copy-start(bf16[640,2560]{1,0:T(8,128)(2,1)} %param.22) | copy-start | bytes 9830404
  7.2 94.2 %copy-start.11 = (bf16[1,8,1280]{2,1,0:T(8,128)(2,1)S(1)}, bf16[1,8,1280]{2,1,0:T(8,128)(2,1)}, u32[]{:S(2)}) copy-start(bf16[1,8,1280]{2,1,0:T(8,128)(2,1)} %param.18) | copy-start | bytes 61444
  7.2 105.0 %reduce-scatter.3.cloned.1.call-start = ((), (), s32[]{:S(2)}) async-start(), calls=%async_computation.5 | async-start | bytes 122880 | tf_op jit(solution)/shard_map/reduce_scatter | solution.py:101
  101.4 5.2 %copy-start.6 = (s32[1,8,2]{1,2,0:T(2,128)S(1)}, s32[1,8,2]{1,2,0:T(2,128)}, u32[]{:S(2)}) copy-start(s32[1,8,2]{1,2,0:T(2,128)} %param.25) | copy-start | bytes 196
  101.4 10.8 %copy-start.5 = (bf16[1,8,2560]{2,1,0:T(8,128)(2,1)S(1)}, bf16[1,8,2560]{2,1,0:T(8,128)(2,1)}, u32[]{:S(2)}) copy-start(bf16[1,8,2560]{2,1,0:T(8,128)(2,1)} %param.21) | copy-start | bytes 122884
  101.4 11.7 %copy-start.8 = (f32[2560]{0:T(1024)S(1)}, f32[2560]{0:T(1024)}, u32[]{:S(2)}) copy-start(f32[2560]{0:T(1024)} %param.23) | copy-start | bytes 30724
  107.0 6.1 %copy-start.9 = (s32[16]{0:T(128)}, s32[16]{0:T(128)S(1)}, u32[]{:S(2)}) copy-start(s32[16]{0:T(128)S(1)} %select_reduce_fusion) | copy-start | bytes 196
  113.1 87.5 %copy-start.3 = (bf16[8,2560]{1,0:T(8,128)(2,1)}, bf16[8,2560]{1,0:T(8,128)(2,1)S(1)}, u32[]{:S(2)}) copy-start(bf16[8,2560]{1,0:T(8,128)(2,1)S(1)} %get-tuple-element.3) | copy-start | bytes 122884
  113.5 40.0 %copy-start.2 = (bf16[1,192,2560]{2,1,0:T(8,128)(2,1)S(1)}, bf16[1,192,2560]{2,1,0:T(8,128)(2,1)}, u32[]{:S(2)}) copy-start(bf16[1,192,2560]{2,1,0:T(8,128)(2,1)} %param.26) | copy-start | bytes 2949124
  152.4 1.1 copy-start.1
  158.7 3.6 %copy-start.10 = (s32[16]{0:T(128)S(1)}, s32[16]{0:T(128)}, u32[]{:S(2)}) copy-start(s32[16]{0:T(128)} %copy-done.9) | copy-start | bytes 196
  158.7 3.7 %copy-start.7 = (s32[1,8,2]{1,2,0:T(2,128)S(1)}, s32[1,8,2]{1,2,0:T(2,128)}, u32[]{:S(2)}) copy-start(s32[1,8,2]{1,2,0:T(2,128)} %param.25) | copy-start | bytes 196
  158.7 4.1 %copy-start.4 = (f32[2560,4]{0,1:T(4,128)S(1)}, f32[2560,4]{0,1:T(4,128)}, u32[]{:S(2)}) copy-start(f32[2560,4]{0,1:T(4,128)} %param.24) | copy-start | bytes 122884
  158.7 35.4 %all-to-all-start.2 = ((bf16[32,8,2560]{2,1,0:T(8,128)(2,1)}), bf16[32,8,2560]{2,1,0:T(8,128)(2,1)}, u32[]{:S(2)}, u32[]{:S(2)}) async-start(bf16[32,8,2560]{2,1,0:T(8,128)(2,1)} %fusion), calls=%async_computation.4 | async-start | bytes 2621440 | tf_op jit(solution)/shard_map/all_to_all | solution.py:150
  162.3 38.4 %reduce-scatter.5.cloned.1.call-start = ((), (), s32[]{:S(2)}) async-start(), calls=%async_computation.6 | async-start | bytes 122880 | tf_op jit(solution)/shard_map/reduce_scatter | solution.py:113
Sparse Core Ops, SparseCore 0:
  106.7 5.4 reduce-scatter.2
  171.4 8.6 reduce-scatter.4
where the time goes:
time: 210 us; the launch traced here: 209 us
  blocking collectives  131 us (62%)
  waiting for transfers between devices  28.1 us (13%)
  matrix products  16.6 us (8%)
  between operations  14.3 us (7%)
  local copies, waits for them, and re-layouts  8.99 us (4%)
  other arithmetic  6.33 us (3%)
  starting transfers between devices  3.6 us (2%)
    all_gather x1, blocking collectives, per_device(): lax.all_gather(stale_keys[0], 'patch', axis=0, tiled=True)  47 us
    all_gather x1, blocking collectives, per_device(): lax.all_gather(stale_values[0], 'patch', axis=0, tiled=True)  39.8 us
    all_to_all x1, blocking collectives, per_device(): lax.all_to_all(send_rows, ('patch', 'image'), split_axis=0, concat_axis=0...  38.8 us
    all_to_all x1, waiting for transfers between devices, per_device(): lax.all_to_all(partial_value, ('patch', 'image'), split_axis=0, concat_ax...  22.9 us
    reduce_scatter x1, waiting for transfers between devices, per_device(): lax.psum_scatter(jnp.dot(block_rows, out_proj, preferred_element_type=jnp...  5.16 us
    dot_general x1, matrix products, expert_part(): jnp.dot(hidden, down_rows, preferred_element_type=jnp.float32)  4.68 us
  transfers between devices with their start and end apart: 3, of which 2 were waited for; matrix products, arithmetic and copies ran while one was open for 7% of the time, Pallas kernels for 0%

commit v1 on v0

v1 whole, which is shorter than its diff:
```python
import functools

import jax
import jax.numpy as jnp
from jax import lax
from jax.experimental import pallas as pl
from jax.experimental.pallas import tpu as pltpu
from jax.sharding import PartitionSpec as P

HD = 128
EPS = 1e-06
MEMBERS = 4
MESH = pl.DeviceIdType.MESH
F32 = jnp.float32
BF16 = jnp.bfloat16


def dot_nt(rows, weight):
    return lax.dot_general(rows, weight, (((1,), (1,)), ((), ())), preferred_element_type=F32)


def dot_nn(rows, weight):
    return lax.dot_general(rows, weight, (((1,), (0,)), ((), ())), preferred_element_type=F32)


def stack_halves(rows):
    width = rows.shape[1] // 2
    return jnp.concatenate([rows[:, :width], rows[:, width:]], axis=0).astype(BF16)


def unstack_halves(packed):
    rows = packed.astype(F32)
    count = rows.shape[0] // 2
    return jnp.concatenate([rows[:count], rows[count:]], axis=1)


def send_count(groups):
    others = groups - 1
    members = MEMBERS - 1
    kv = 4 + 2 * others + 2 * groups * members
    tokens = 1 + others + groups * members + groups * MEMBERS - 1
    results = 1 + groups + groups * members + 2 * others + 1
    return kv + tokens + results


def kernel(
    groups,
    q_ref, fk_ref, fv_ref, sk_ref, sv_ref, res_ref, gain_ref, router_ref, ids_ref,
    wo_hbm, rg_hbm, ru_hbm, rd_hbm, sg_hbm, su_hbm, sd_hbm,
    att_ref, out_ref,
    wo, rg, ru, rd, sg, su, sd,
    stale_own, sib_kv, sib_q, sib_res, q_x, res_x, kv,
    part_s, part_r, tok, sh_s, sh_r,
    half_s, half_r, half_own, plane_s, plane_r, line_s, line_r,
    w_sem, send_sem, sib_sem, kv_sem, tok_sem, toks_sem, half_sem, plane_sem, line_sem,
):
    patch = lax.axis_index("patch")
    core = lax.axis_index("image")
    other = 1 - core
    first = core == 0
    group = patch // MEMBERS
    member = patch % MEMBERS
    rows = q_ref.shape[1]
    heads_half = q_ref.shape[2] // 2
    width = res_ref.shape[2]
    half = width // 2

    def at(step_group, step_member, to_core):
        target = ((group + step_group) % groups) * MEMBERS + (member + step_member) % MEMBERS
        return {"patch": target, "image": to_core}

    sibling = at(0, 0, other)

    barrier = pltpu.get_barrier_semaphore()
    greeted = [sibling]
    for d in range(1, groups):
        greeted += [at(d, 0, core), at(d, 0, other)]
    for k in range(1, MEMBERS):
        greeted.append(at(0, k, core))
    for target in greeted:
        pl.semaphore_signal(barrier, inc=1, device_id=target, device_id_type=MESH)

    weights = []
    pairs = [(wo_hbm, wo), (sg_hbm, sg), (su_hbm, su), (sd_hbm, sd)]
    pairs += [(rg_hbm, rg), (ru_hbm, ru), (rd_hbm, rd)]
    for number, (src, dst) in enumerate(pairs):
        copy = pltpu.make_async_copy(src, dst, w_sem.at[number])
        copy.start()
        weights.append(copy)

    sent = []

    def send(src, dst, recv, target):
        copy = pltpu.make_async_remote_copy(
            src_ref=src, dst_ref=dst, send_sem=send_sem.at[len(sent)], recv_sem=recv,
            device_id=target, device_id_type=MESH,
        )
        copy.start()
        sent.append(copy)

    def arrived(ref, recv):
        pltpu.make_async_remote_copy(
            src_ref=ref, dst_ref=ref, send_sem=send_sem.at[0], recv_sem=recv,
            device_id=sibling, device_id_type=MESH,
        ).wait_recv()

    def split(ref):
        whole = ref[0].astype(F32)
        left, right = whole[:, :heads_half], whole[:, heads_half:]
        return jnp.where(first, left, right), jnp.where(first, right, left)

    sk_mine, sk_theirs = split(sk_ref)
    sv_mine, sv_theirs = split(sv_ref)
    stale_own[0] = jnp.concatenate([sk_mine, sv_mine], axis=0).astype(BF16)
    sib_kv[0] = jnp.concatenate([sk_theirs, sv_theirs], axis=0).astype(BF16)
    fk_mine, fk_theirs = split(fk_ref)
    fv_mine, fv_theirs = split(fv_ref)
    kv[0, 0, 0] = jnp.concatenate([fk_mine, fv_mine], axis=0).astype(BF16)
    sib_kv[1] = jnp.concatenate([fk_theirs, fv_theirs], axis=0).astype(BF16)
    q_mine, q_theirs = split(q_ref)
    sib_q[...] = q_theirs
    residual = res_ref[0].astype(F32)
    sib_res[...] = residual

    pl.semaphore_wait(barrier, len(greeted))

    send(sib_kv.at[0], stale_own.at[1], sib_sem.at[0], sibling)
    for d in range(1, groups):
        send(stale_own.at[0], kv.at[groups - d, 0, 0], kv_sem.at[groups - d, 0, 0], at(d, 0, core))
        send(sib_kv.at[0], kv.at[groups - d, 0, 1], kv_sem.at[groups - d, 0, 1], at(d, 0, other))
    for k in range(1, MEMBERS):
        send(stale_own.at[0], kv.at[0, MEMBERS - k, 0], kv_sem.at[0, MEMBERS - k, 0], at(0, k, core))
    send(sib_kv.at[1], kv.at[0, 0, 1], kv_sem.at[0, 0, 1], sibling)
    send(sib_q, q_x, sib_sem.at[1], sibling)
    send(sib_res, res_x, sib_sem.at[2], sibling)
    arrived(stale_own.at[1], sib_sem.at[0])
    for k in range(1, MEMBERS):
        send(stale_own.at[1], kv.at[0, MEMBERS - k, 1], kv_sem.at[0, MEMBERS - k, 1], at(0, k, core))
    for d in range(1, groups):
        for i in range(2):
            arrived(kv.at[d, 0, i], kv_sem.at[d, 0, i])
            for k in range(1, MEMBERS):
                send(kv.at[d, 0, i], kv.at[d, MEMBERS - k, i], kv_sem.at[d, MEMBERS - k, i],
                     at(0, k, core))
    arrived(q_x, sib_sem.at[1])
    arrived(res_x, sib_sem.at[2])
    arrived(kv.at[0, 0, 1], kv_sem.at[0, 0, 1])
    for d in range(groups):
        for k in range(1, MEMBERS):
            for i in range(2):
                arrived(kv.at[d, k, i], kv_sem.at[d, k, i])

    heads = heads_half // HD
    key_rows = groups * MEMBERS * 2 * rows
    row_head = lax.broadcasted_iota(jnp.int32, (heads * rows, heads_half), 0) // rows
    lane_head = lax.broadcasted_iota(jnp.int32, (heads * rows, heads_half), 1) // HD
    own_head = row_head == lane_head
    is_key = lax.broadcasted_iota(jnp.int32, (heads * rows, key_rows), 1) % (2 * rows) < rows
    outs = []
    for i, query in enumerate((q_mine, q_x[...])):
        block = kv[:, :, i].reshape(key_rows, heads_half)
        spread = jnp.where(own_head, jnp.concatenate([query] * heads, axis=0), 0.0).astype(BF16)
        scores = dot_nt(spread, block) * (HD ** -0.5)
        scores = jnp.where(is_key, scores, -1e30)
        top = jnp.max(scores, axis=-1, keepdims=True)
        exp_scores = jnp.where(is_key, jnp.exp(scores - top), 0.0)
        total = jnp.sum(exp_scores, axis=-1, keepdims=True)
        moved = pltpu.roll(exp_scores, rows, axis=1).astype(BF16)
        mixed = dot_nn(moved, block) / total
        outs.append(jnp.concatenate(
            [mixed[h * rows:(h + 1) * rows, h * HD:(h + 1) * HD] for h in range(heads)], axis=1))

    def by_image(mine, theirs):
        return jnp.concatenate(
            [jnp.where(first, mine, theirs), jnp.where(first, theirs, mine)], axis=0)

    def own_rows(both):
        return jnp.where(first, both[:rows], both[rows:])

    def other_rows(both):
        return jnp.where(first, both[rows:], both[:rows])

    weights[0].wait()
    part_s[...] = dot_nn(by_image(outs[0], outs[1]).astype(BF16), wo[...])
    send(part_s, part_r, sib_sem.at[3], sibling)
    arrived(part_r, sib_sem.at[3])
    projected = part_s[...] + part_r[...]
    attended = (by_image(residual, res_x[...]) + projected).astype(BF16).astype(F32)
    mean_sq = jnp.mean(attended * attended, axis=-1, keepdims=True)
    normed32 = attended * lax.rsqrt(mean_sq + EPS) * gain_ref[...]
    normed = normed32.astype(BF16)
    tok[0, 0, 0] = normed[:, :half]
    tok[0, 0, 1] = normed[:, half:]

    own = tok.at[0, 0, core]
    for d in range(1, groups):
        send(own, tok.at[groups - d, 0, core], tok_sem.at[groups - d, 0], at(d, 0, core))
    for k in range(1, MEMBERS):
        send(own, tok.at[0, MEMBERS - k, core], tok_sem.at[0, MEMBERS - k], at(0, k, core))

    mid = own_rows(attended)
    att_ref[0] = mid.astype(BF16)
    for number in (1, 2, 3):
        weights[number].wait()
    hidden = jax.nn.silu(dot_nt(normed, sg[...])) * dot_nt(normed, su[...])
    shared = dot_nn(hidden.astype(BF16), sd[...])
    sh_s[...] = stack_halves(other_rows(shared))
    send(sh_s, sh_r, sib_sem.at[4], sibling)

    for d in range(1, groups):
        arrived(tok.at[d, 0, core], tok_sem.at[d, 0])
        for k in range(1, MEMBERS):
            send(tok.at[d, 0, core], tok.at[d, MEMBERS - k, core], tok_sem.at[d, MEMBERS - k],
                 at(0, k, core))
        send(tok.at[d, 0, core], tok.at[d, 0, core], toks_sem.at[d, 0], sibling)

    mine_normed = own_rows(normed.astype(F32))
    logits = lax.dot_general(mine_normed, router_ref[...], (((1,), (1,)), ((), ())),
                             precision=lax.Precision.HIGHEST, preferred_element_type=F32)
    probs = jax.nn.sigmoid(logits)
    experts = lax.broadcasted_iota(jnp.int32, (rows, groups), 1)
    ids = ids_ref[0]
    named = (ids[:, 0:1] == experts) | (ids[:, 1:2] == experts)
    pair_weight = jnp.where(named, probs, 0.0)
    base = mid + own_rows(shared)

    for number in (4, 5, 6):
        weights[number].wait()

    def expert(d):
        for k in range(1, MEMBERS):
            arrived(tok.at[d, k, core], tok_sem.at[d, k])
            send(tok.at[d, k, core], tok.at[d, k, core], toks_sem.at[d, k], sibling)
        for k in range(MEMBERS):
            if d or k:
                arrived(tok.at[d, k, other], toks_sem.at[d, k])
        count = MEMBERS * 2 * rows
        left = tok[d, :, 0].reshape(count, half)
        right = tok[d, :, 1].reshape(count, half)
        gate = dot_nt(left, rg[:, :half]) + dot_nt(right, rg[:, half:])
        up = dot_nt(left, ru[:, :half]) + dot_nt(right, ru[:, half:])
        inner = (jax.nn.silu(gate) * up).astype(BF16)
        out_left = dot_nn(inner, rd[:, :half])
        out_right = dot_nn(inner, rd[:, half:])
        half_own[d] = jnp.where(first, out_left, out_right)
        half_s[d] = jnp.where(first, out_right, out_left).astype(BF16)
        send(half_s.at[d], half_r.at[d], half_sem.at[d], sibling)

    def to_plane(d):
        arrived(half_r.at[d], half_sem.at[d])
        half_own[d] += half_r[d].astype(F32)
        for k in range(1, MEMBERS):
            plane_s[d, k] = half_own[d, pl.ds(k * 2 * rows, 2 * rows)].astype(BF16)
            send(plane_s.at[d, k], plane_r.at[d, MEMBERS - k], plane_sem.at[d, MEMBERS - k],
                 at(0, k, core))

    def to_line(d):
        total = half_own[d, pl.ds(0, 2 * rows)]
        for k in range(1, MEMBERS):
            arrived(plane_r.at[d, k], plane_sem.at[d, k])
            total += plane_r[d, k].astype(F32)
        line_s[d, 1] = stack_halves(other_rows(total))
        back = (groups - d) % groups
        if d == 0:
            line_r[0, core] = stack_halves(own_rows(total))
        else:
            line_s[d, 0] = stack_halves(own_rows(total))
            send(line_s.at[d, 0], line_r.at[back, core], line_sem.at[back, core], at(d, 0, core))
        send(line_s.at[d, 1], line_r.at[back, core], line_sem.at[back, core], at(d, 0, other))

    order = list(range(groups))
    for step in range(groups + 2):
        if step < groups:
            expert(order[step])
        if 0 <= step - 1 < groups:
            to_plane(order[step - 1])
        if 0 <= step - 2 < groups:
            to_line(order[step - 2])

    arrived(sh_r, sib_sem.at[4])
    result = base + unstack_halves(sh_r[...])
    for d in order:
        if d == 0:
            arrived(line_r.at[0, other], line_sem.at[0, other])
        else:
            arrived(line_r.at[d, 0], line_sem.at[d, 0])
            arrived(line_r.at[d, 1], line_sem.at[d, 1])
        column = jnp.where(experts == (group + d) % groups, pair_weight, 0.0)
        scale = jnp.sum(column, axis=1, keepdims=True)
        value = jnp.concatenate(
            [unstack_halves(line_r[d, 0]), unstack_halves(line_r[d, 1])], axis=1)
        result += scale * value
    out_ref[0] = result.astype(BF16)

    for copy in sent:
        copy.wait_send()


def per_device(
    queries, fresh_keys, fresh_values, stale_keys, stale_values, residual, out_proj, norm_gain,
    router, expert_ids, routed_gate, routed_up, routed_down, shared_gate, shared_up, shared_down,
):
    groups = router.shape[1]
    rows, width = residual.shape[1:]
    half = width // 2
    heads_half = queries.shape[2] // 2
    pack = 2 * rows
    weights = (out_proj, routed_gate[0], routed_up[0], routed_down[0],
               shared_gate, shared_up, shared_down)
    order = (0, 1, 2, 3, 4, 5, 6)
    vmem = pl.BlockSpec(memory_space=pltpu.VMEM)
    hbm = pl.BlockSpec(memory_space=pl.ANY)
    dma = pltpu.SemaphoreType.DMA
    scratch = [pltpu.VMEM(weights[n].shape, BF16) for n in order]
    scratch += [
        pltpu.VMEM((2, pack, heads_half), BF16),
        pltpu.VMEM((2, pack, heads_half), BF16),
        pltpu.VMEM((rows, heads_half), F32),
        pltpu.VMEM((rows, width), F32),
        pltpu.VMEM((rows, heads_half), F32),
        pltpu.VMEM((rows, width), F32),
        pltpu.VMEM((groups, MEMBERS, 2, pack, heads_half), BF16),
        pltpu.VMEM((pack, width), F32),
        pltpu.VMEM((pack, width), F32),
        pltpu.VMEM((groups, MEMBERS, 2, pack, half), BF16),
        pltpu.VMEM((pack, half), BF16),
        pltpu.VMEM((pack, half), BF16),
        pltpu.VMEM((groups, MEMBERS * pack, half), BF16),
        pltpu.VMEM((groups, MEMBERS * pack, half), BF16),
        pltpu.VMEM((groups, MEMBERS * pack, half), F32),
        pltpu.VMEM((groups, MEMBERS, pack, half), BF16),
        pltpu.VMEM((groups, MEMBERS, pack, half), BF16),
        pltpu.VMEM((groups, 2, pack, half // 2), BF16),
        pltpu.VMEM((groups, 2, pack, half // 2), BF16),
        dma((7,)),
        dma((send_count(groups),)),
        dma((5,)),
        dma((groups, MEMBERS, 2)),
        dma((groups, MEMBERS)),
        dma((groups, MEMBERS)),
        dma((groups,)),
        dma((groups, MEMBERS)),
        dma((groups, 2)),
    ]
    return pl.pallas_call(
        functools.partial(kernel, groups),
        out_shape=(
            jax.ShapeDtypeStruct(residual.shape, BF16),
            jax.ShapeDtypeStruct(residual.shape, BF16),
        ),
        in_specs=[vmem] * 9 + [hbm] * 7,
        out_specs=(vmem, vmem),
        scratch_shapes=scratch,
        compiler_params=pltpu.CompilerParams(
            collective_id=0, has_side_effects=True, vmem_limit_bytes=56 * 1024 * 1024
        ),
        name="block",
    )(
        queries, fresh_keys, fresh_values, stale_keys, stale_values, residual,
        norm_gain.reshape(1, width), router.T, expert_ids, *weights,
    )


def solution(mesh):
    tokens = P(("groups", "image"), "patch", None)
    in_specs = (
        (tokens,) * 6
        + (P("image", None), P(), P(), tokens)
        + (P("patch", "image", None),) * 3
        + (P("image", None),) * 3
    )
    return jax.shard_map(
        per_device, mesh=mesh, in_specs=in_specs, out_specs=(tokens, tokens), check_vma=False
    )
```

time: 210 us -> 55 us (0.26)
  blocking collectives: 131 us -> 0 us
  Pallas kernels: 0 us -> 48.6 us
  waiting for transfers between devices: 28.1 us -> 0 us
  matrix products: 16.6 us -> 0 us
  between operations: 14.3 us -> 0.64 us
  other arithmetic: 6.33 us -> 0 us
  starting transfers between devices: 3.6 us -> 0 us
  local copies, waits for them, and re-layouts: 8.99 us -> 5.45 us
    all_gather x3 -> x0, blocking collectives: 88.6 us -> none  [the longest x1 47 us: per_device(): lax.all_gather(stale_keys[0], 'patch', axis=0, tiled=True)]
    pallas_call x0 -> x1, Pallas kernels: none -> 48.6 us  [per_device(): pl.pallas_call(functools.partial(kernel, groups), out_shape=(jax.ShapeDty...]
    all_to_all x2 -> x0, blocking collectives: 42.5 us -> none  [the longest x1 38.8 us: per_device(): lax.all_to_all(send_rows, ('patch', 'image'), split_axis=0, concat_axis=0...]
    all_to_all x1 -> x0, waiting for transfers between devices: 22.9 us -> none  [per_device(): lax.all_to_all(partial_value, ('patch', 'image'), split_axis=0, concat_ax...]
    dot_general x11 -> x0, matrix products: 16.6 us -> none  [the longest x1 4.68 us: expert_part(): jnp.dot(hidden, down_rows, preferred_element_type=jnp.float32)]
    reduce_scatter x2 -> x0, waiting for transfers between devices: 5.17 us -> none  [the longest x1 5.16 us: per_device(): lax.psum_scatter(jnp.dot(block_rows, out_proj, preferred_element_type=jnp...]
    reduce_sum x7 -> x0, other arithmetic: 4.55 us -> none  [the longest x1 2.27 us: per_device(): jnp.sum(returned.reshape(num_experts, per_expert, capacity, model_width)....]
    all_gather x2 -> x0, local copies, waits for them, and re-layouts: 3.74 us -> none  [the longest x1 1.87 us: per_device(): lax.all_gather(stale_keys[0], 'patch', axis=0, tiled=True)]
  transfers between devices with their start and end apart: 3 -> 0, of which waited for: 2 -> 0; matrix products, arithmetic and copies ran while one was open for 7% -> 0% of each run, Pallas kernels for 0% -> 0%
where the time goes in v1:
time: 55 us; the launch traced here: 54.6 us
  Pallas kernels  48.6 us (88%)
  local copies, waits for them, and re-layouts  5.45 us (10%)
  between operations  0.64 us (1%)
    pallas_call x1, Pallas kernels, per_device(): pl.pallas_call(functools.partial(kernel, groups), out_shape=(jax.ShapeDty...  48.6 us
    unnamed x3, local copies, waits for them, and re-layouts  4.14 us
    reshape x1, local copies, waits for them, and re-layouts, per_device(): norm_gain.reshape(1, width)  1.31 us

profile of v1, /device:TPU:0, one launch (start us, length us, event | category | flops | bytes accessed | tf_op | source)
XLA Modules:
  0.0 54.6 jit_solution(10060529374472857692)
XLA Ops:
  0.6 1.3 %copy.18.ids_ref = s32[1,8,2]{2,1,0:T(8,128)} copy(s32[1,8,2]{1,2,0:T(2,128)} %param.25) | data formatting | bytes 128 | tf_op args[9]
  2.0 1.3 %reshape.7.gain_ref = f32[1,2560]{1,0:T(1,128)} reshape(f32[2560]{0:T(1024)} %param.23) | data formatting | bytes 20480 | tf_op jit(solution)/shard_map/reshape | solution.py:360
  3.3 48.6 %block.1 = (bf16[1,8,2560]{2,1,0:T(8,128)(2,1)}, bf16[1,8,2560]{2,1,0:T(8,128)(2,1)}) custom-call(bf16[1,8,1280]{2,1,0:T(8,128)(2,1)} %q_ref.1, bf16[1,8,1280]{2,1,0:T(8,128)(2,1)} %fk_ref.1, bf16[1,8,1280]{2,1,0:T(8,128)(2,1)} %fv_ref.1, bf16[1,8,1280]{2,1,0:T(8,128)(2,1)} %sk_ref.1, bf16[1,8,1280]{2,1,0:T(8,128)(2,1)} %sv_ref.1, ...), custom_call_target="tpu_custom_call" | custom-call | tf_op jit(solution)/shard_map/block/pallas_call | solution.py:345
  51.8 1.4 %copy.21 = bf16[1,8,2560]{2,1,0:T(8,128)(2,1)} copy(bf16[1,8,2560]{2,1,0:T(8,128)(2,1)} %get-tuple-element.4) | data formatting | bytes 81920
  53.2 1.4 %copy.22 = bf16[1,8,2560]{2,1,0:T(8,128)(2,1)} copy(bf16[1,8,2560]{2,1,0:T(8,128)(2,1)} %get-tuple-element.5) | data formatting | bytes 81920

commit v2 on v1

--- a/solution.py
+++ b/solution.py
@@ -37,22 +37,23 @@
 def send_count(groups):
     others = groups - 1
     members = MEMBERS - 1
-    kv = 4 + 2 * others + 2 * groups * members
-    tokens = 1 + others + groups * members + groups * MEMBERS - 1
+    kv = 4 + 2 * others + 2 * groups * members + others * members
+    tokens = 1 + others + groups * members + others * members + groups * MEMBERS - 1
     results = 1 + groups + groups * members + 2 * others + 1
     return kv + tokens + results
 
 
 def kernel(
     groups,
-    q_ref, fk_ref, fv_ref, sk_ref, sv_ref, res_ref, gain_ref, router_ref, ids_ref,
+    q_hbm, fk_hbm, fv_hbm, sk_hbm, sv_hbm, res_hbm, gain_hbm, router_hbm, ids_hbm,
     wo_hbm, rg_hbm, ru_hbm, rd_hbm, sg_hbm, su_hbm, sd_hbm,
     att_ref, out_ref,
+    q_ref, fk_ref, fv_ref, sk_ref, sv_ref, res_ref, gain_ref, router_ref, ids_ref,
     wo, rg, ru, rd, sg, su, sd,
     stale_own, sib_kv, sib_q, sib_res, q_x, res_x, kv,
     part_s, part_r, tok, sh_s, sh_r,
     half_s, half_r, half_own, plane_s, plane_r, line_s, line_r,
-    w_sem, send_sem, sib_sem, kv_sem, tok_sem, toks_sem, half_sem, plane_sem, line_sem,
+    in_sem, w_sem, send_sem, sib_sem, kv_sem, rest_sem, tok_sem, tokr_sem, toks_sem, half_sem, plane_sem, line_sem,
 ):
     patch = lax.axis_index("patch")
     core = lax.axis_index("image")
@@ -71,14 +72,31 @@
 
     sibling = at(0, 0, other)
 
+    near = jnp.minimum(group, groups - 1 - group)
+    forward = 1 - 2 * ((2 * group) // groups)
+    steps = [0]
+    for s in range(groups - 1):
+        both = forward * (1 - 2 * (s % 2)) * (s // 2 + 1)
+        rest = forward * (s - near + 1)
+        steps.append((jnp.where(s < 2 * near, both, rest) + groups) % groups)
+
     barrier = pltpu.get_barrier_semaphore()
     greeted = [sibling]
     for d in range(1, groups):
         greeted += [at(d, 0, core), at(d, 0, other)]
     for k in range(1, MEMBERS):
-        greeted.append(at(0, k, core))
+        greeted += [at(0, k, core), at(0, k, other)]
     for target in greeted:
         pl.semaphore_signal(barrier, inc=1, device_id=target, device_id_type=MESH)
+
+    loads = []
+    pairs = [(sk_hbm, sk_ref), (sv_hbm, sv_ref), (fk_hbm, fk_ref), (fv_hbm, fv_ref)]
+    pairs += [(q_hbm, q_ref), (res_hbm, res_ref), (gain_hbm, gain_ref)]
+    pairs += [(router_hbm, router_ref), (ids_hbm, ids_ref)]
+    for number, (src, dst) in enumerate(pairs):
+        copy = pltpu.make_async_copy(src, dst, in_sem.at[number])
+        copy.start()
+        loads.append(copy)
 
     weights = []
     pairs = [(wo_hbm, wo), (sg_hbm, sg), (su_hbm, su), (sd_hbm, sd)]
@@ -109,10 +127,14 @@
         left, right = whole[:, :heads_half], whole[:, heads_half:]
         return jnp.where(first, left, right), jnp.where(first, right, left)
 
+    loads[0].wait()
+    loads[1].wait()
     sk_mine, sk_theirs = split(sk_ref)
     sv_mine, sv_theirs = split(sv_ref)
-    stale_own[0] = jnp.concatenate([sk_mine, sv_mine], axis=0).astype(BF16)
+    stale_own[...] = jnp.concatenate([sk_mine, sv_mine], axis=0).astype(BF16)
     sib_kv[0] = jnp.concatenate([sk_theirs, sv_theirs], axis=0).astype(BF16)
+    for load in loads[2:]:
+        load.wait()
     fk_mine, fk_theirs = split(fk_ref)
     fv_mine, fv_theirs = split(fv_ref)
     kv[0, 0, 0] = jnp.concatenate([fk_mine, fv_mine], axis=0).astype(BF16)
@@ -124,31 +146,48 @@
 
     pl.semaphore_wait(barrier, len(greeted))
 
-    send(sib_kv.at[0], stale_own.at[1], sib_sem.at[0], sibling)
-    for d in range(1, groups):
-        send(stale_own.at[0], kv.at[groups - d, 0, 0], kv_sem.at[groups - d, 0, 0], at(d, 0, core))
+    cut = heads_half - heads_half // 5
+    for d in steps[1:]:
+        send(stale_own, kv.at[groups - d, 0, 0], kv_sem.at[groups - d, 0, 0], at(d, 0, core))
         send(sib_kv.at[0], kv.at[groups - d, 0, 1], kv_sem.at[groups - d, 0, 1], at(d, 0, other))
     for k in range(1, MEMBERS):
-        send(stale_own.at[0], kv.at[0, MEMBERS - k, 0], kv_sem.at[0, MEMBERS - k, 0], at(0, k, core))
+        back = MEMBERS - k
+        send(stale_own, kv.at[0, back, 0], kv_sem.at[0, back, 0], at(0, k, core))
+        send(sib_kv.at[0], kv.at[0, back, 1], kv_sem.at[0, back, 1], at(0, k, other))
     send(sib_kv.at[1], kv.at[0, 0, 1], kv_sem.at[0, 0, 1], sibling)
     send(sib_q, q_x, sib_sem.at[1], sibling)
     send(sib_res, res_x, sib_sem.at[2], sibling)
-    arrived(stale_own.at[1], sib_sem.at[0])
-    for k in range(1, MEMBERS):
-        send(stale_own.at[1], kv.at[0, MEMBERS - k, 1], kv_sem.at[0, MEMBERS - k, 1], at(0, k, core))
-    for d in range(1, groups):
+
+    def kv_part(d, k, i):
+        return kv.at[d, k, i, :, pl.ds(0, cut)]
+
+    def kv_rest(d, k):
+        return kv.at[d, k, :, :, pl.ds(cut, heads_half - cut)]
+
+    def kv_on(d):
         for i in range(2):
             arrived(kv.at[d, 0, i], kv_sem.at[d, 0, i])
             for k in range(1, MEMBERS):
-                send(kv.at[d, 0, i], kv.at[d, MEMBERS - k, i], kv_sem.at[d, MEMBERS - k, i],
-                     at(0, k, core))
+                back = MEMBERS - k
+                send(kv_part(d, 0, i), kv_part(d, back, i), kv_sem.at[d, back, i], at(0, k, core))
+
+    for d in steps[1:2]:
+        kv_on(d)
+    for k in range(1, MEMBERS):
+        for i in range(2):
+            arrived(kv.at[0, k, i], kv_sem.at[0, k, i])
+        for d in steps[1:]:
+            send(kv_rest(0, k), kv_rest(groups - d, k), rest_sem.at[groups - d, k], at(d, 0, core))
+    for d in steps[2:]:
+        kv_on(d)
     arrived(q_x, sib_sem.at[1])
     arrived(res_x, sib_sem.at[2])
     arrived(kv.at[0, 0, 1], kv_sem.at[0, 0, 1])
-    for d in range(groups):
+    for d in steps[1:]:
         for k in range(1, MEMBERS):
             for i in range(2):
-                arrived(kv.at[d, k, i], kv_sem.at[d, k, i])
+                arrived(kv_part(d, k, i), kv_sem.at[d, k, i])
+            arrived(kv_rest(d, k), rest_sem.at[d, k])
 
     heads = heads_half // HD
     key_rows = groups * MEMBERS * 2 * rows
@@ -187,13 +226,13 @@
     projected = part_s[...] + part_r[...]
     attended = (by_image(residual, res_x[...]) + projected).astype(BF16).astype(F32)
     mean_sq = jnp.mean(attended * attended, axis=-1, keepdims=True)
-    normed32 = attended * lax.rsqrt(mean_sq + EPS) * gain_ref[...]
+    normed32 = attended * lax.rsqrt(mean_sq + EPS) * gain_ref[...].reshape(1, width)
     normed = normed32.astype(BF16)
     tok[0, 0, 0] = normed[:, :half]
     tok[0, 0, 1] = normed[:, half:]
 
     own = tok.at[0, 0, core]
-    for d in range(1, groups):
+    for d in steps[1:]:
         send(own, tok.at[groups - d, 0, core], tok_sem.at[groups - d, 0], at(d, 0, core))
     for k in range(1, MEMBERS):
         send(own, tok.at[0, MEMBERS - k, core], tok_sem.at[0, MEMBERS - k], at(0, k, core))
@@ -207,46 +246,76 @@
     sh_s[...] = stack_halves(other_rows(shared))
     send(sh_s, sh_r, sib_sem.at[4], sibling)
 
-    for d in range(1, groups):
+    tok_cut = half - half // 5
+
+    def tok_part(d, k):
+        return tok.at[d, k, core, :, pl.ds(0, tok_cut)]
+
+    def tok_rest(d, k):
+        return tok.at[d, k, core, :, pl.ds(tok_cut, half - tok_cut)]
+
+    def tok_on(d):
         arrived(tok.at[d, 0, core], tok_sem.at[d, 0])
         for k in range(1, MEMBERS):
-            send(tok.at[d, 0, core], tok.at[d, MEMBERS - k, core], tok_sem.at[d, MEMBERS - k],
-                 at(0, k, core))
+            back = MEMBERS - k
+            send(tok_part(d, 0), tok_part(d, back), tok_sem.at[d, back], at(0, k, core))
         send(tok.at[d, 0, core], tok.at[d, 0, core], toks_sem.at[d, 0], sibling)
 
+    for d in steps[1:2]:
+        tok_on(d)
+    for k in range(1, MEMBERS):
+        arrived(tok.at[0, k, core], tok_sem.at[0, k])
+        for d in steps[1:]:
+            back = groups - d
+            send(tok_rest(0, k), tok_rest(back, k), tokr_sem.at[back, k], at(d, 0, core))
+        send(tok.at[0, k, core], tok.at[0, k, core], toks_sem.at[0, k], sibling)
+    for d in steps[2:]:
+        tok_on(d)
+
     mine_normed = own_rows(normed.astype(F32))
-    logits = lax.dot_general(mine_normed, router_ref[...], (((1,), (1,)), ((), ())),
+    logits = lax.dot_general(router_ref[...], mine_normed, (((1,), (1,)), ((), ())),
                              precision=lax.Precision.HIGHEST, preferred_element_type=F32)
     probs = jax.nn.sigmoid(logits)
-    experts = lax.broadcasted_iota(jnp.int32, (rows, groups), 1)
+    experts = lax.broadcasted_iota(jnp.int32, (groups, rows), 0)
     ids = ids_ref[0]
-    named = (ids[:, 0:1] == experts) | (ids[:, 1:2] == experts)
+    named = (ids[0:1] == experts) | (ids[1:2] == experts)
     pair_weight = jnp.where(named, probs, 0.0)
+    diagonal = (lax.broadcasted_iota(jnp.int32, (rows, rows), 0)
+                == lax.broadcasted_iota(jnp.int32, (rows, rows), 1))
     base = mid + own_rows(shared)
 
     for number in (4, 5, 6):
         weights[number].wait()
 
-    def expert(d):
+    def pass_on(s):
+        d = steps[s]
         for k in range(1, MEMBERS):
-            arrived(tok.at[d, k, core], tok_sem.at[d, k])
+            arrived(tok_part(d, k), tok_sem.at[d, k])
+            arrived(tok_rest(d, k), tokr_sem.at[d, k])
             send(tok.at[d, k, core], tok.at[d, k, core], toks_sem.at[d, k], sibling)
-        for k in range(MEMBERS):
-            if d or k:
-                arrived(tok.at[d, k, other], toks_sem.at[d, k])
-        count = MEMBERS * 2 * rows
-        left = tok[d, :, 0].reshape(count, half)
-        right = tok[d, :, 1].reshape(count, half)
+
+    def expert(slots, wanted):
+        for s in wanted:
+            for k in range(MEMBERS):
+                if s or k:
+                    arrived(tok.at[steps[s], k, other], toks_sem.at[steps[s], k])
+        low, high = slots
+        count = (high - low) * MEMBERS * 2 * rows
+        left = tok[low:high, :, 0].reshape(count, half)
+        right = tok[low:high, :, 1].reshape(count, half)
         gate = dot_nt(left, rg[:, :half]) + dot_nt(right, rg[:, half:])
         up = dot_nt(left, ru[:, :half]) + dot_nt(right, ru[:, half:])
         inner = (jax.nn.silu(gate) * up).astype(BF16)
-        out_left = dot_nn(inner, rd[:, :half])
-        out_right = dot_nn(inner, rd[:, half:])
-        half_own[d] = jnp.where(first, out_left, out_right)
-        half_s[d] = jnp.where(first, out_right, out_left).astype(BF16)
-        send(half_s.at[d], half_r.at[d], half_sem.at[d], sibling)
-
-    def to_plane(d):
+        theirs = dot_nn(inner, rd[:, pl.ds(pl.multiple_of(other * half, 128), half)])
+        half_s[low:high] = theirs.astype(BF16).reshape(high - low, -1, half)
+        for s in wanted:
+            d = steps[s]
+            send(half_s.at[d], half_r.at[d], half_sem.at[d], sibling)
+        mine = dot_nn(inner, rd[:, pl.ds(pl.multiple_of(core * half, 128), half)])
+        half_own[low:high] = mine.reshape(high - low, -1, half)
+
+    def to_plane(s):
+        d = steps[s]
         arrived(half_r.at[d], half_sem.at[d])
         half_own[d] += half_r[d].astype(F32)
         for k in range(1, MEMBERS):
@@ -254,39 +323,44 @@
             send(plane_s.at[d, k], plane_r.at[d, MEMBERS - k], plane_sem.at[d, MEMBERS - k],
                  at(0, k, core))
 
-    def to_line(d):
+    def to_line(s):
+        d = steps[s]
         total = half_own[d, pl.ds(0, 2 * rows)]
         for k in range(1, MEMBERS):
             arrived(plane_r.at[d, k], plane_sem.at[d, k])
             total += plane_r[d, k].astype(F32)
         line_s[d, 1] = stack_halves(other_rows(total))
         back = (groups - d) % groups
-        if d == 0:
+        if s == 0:
             line_r[0, core] = stack_halves(own_rows(total))
         else:
             line_s[d, 0] = stack_halves(own_rows(total))
             send(line_s.at[d, 0], line_r.at[back, core], line_sem.at[back, core], at(d, 0, core))
         send(line_s.at[d, 1], line_r.at[back, core], line_sem.at[back, core], at(d, 0, other))
 
-    order = list(range(groups))
-    for step in range(groups + 2):
-        if step < groups:
-            expert(order[step])
-        if 0 <= step - 1 < groups:
-            to_plane(order[step - 1])
-        if 0 <= step - 2 < groups:
-            to_line(order[step - 2])
+    far_first = list(range(groups - 1, 0, -1))
+    expert((0, 1), [0])
+    for s in range(1, groups):
+        pass_on(s)
+    to_plane(0)
+    expert((1, groups), far_first)
+    for s in far_first:
+        to_plane(s)
+    to_line(0)
+    for s in far_first:
+        to_line(s)
 
     arrived(sh_r, sib_sem.at[4])
     result = base + unstack_halves(sh_r[...])
-    for d in order:
-        if d == 0:
+    for s, d in enumerate(steps):
+        if s == 0:
             arrived(line_r.at[0, other], line_sem.at[0, other])
         else:
             arrived(line_r.at[d, 0], line_sem.at[d, 0])
             arrived(line_r.at[d, 1], line_sem.at[d, 1])
-        column = jnp.where(experts == (group + d) % groups, pair_weight, 0.0)
-        scale = jnp.sum(column, axis=1, keepdims=True)
+        named_row = jnp.where(experts == (group + d) % groups, pair_weight, 0.0)
+        named_row = jnp.sum(named_row, axis=0, keepdims=True)
+        scale = jnp.sum(jnp.where(diagonal, named_row, 0.0), axis=1, keepdims=True)
         value = jnp.concatenate(
             [unstack_halves(line_r[d, 0]), unstack_halves(line_r[d, 1])], axis=1)
         result += scale * value
@@ -294,6 +368,11 @@
 
     for copy in sent:
         copy.wait_send()
+
+
+def finish(attended, block_out, att_ref, out_ref):
+    att_ref[...] = attended[...]
+    out_ref[...] = block_out[...]
 
 
 def per_device(
@@ -311,9 +390,12 @@
     vmem = pl.BlockSpec(memory_space=pltpu.VMEM)
     hbm = pl.BlockSpec(memory_space=pl.ANY)
     dma = pltpu.SemaphoreType.DMA
-    scratch = [pltpu.VMEM(weights[n].shape, BF16) for n in order]
+    inputs = (queries, fresh_keys, fresh_values, stale_keys, stale_values, residual,
+              norm_gain, router.T, jnp.transpose(expert_ids, (0, 2, 1)))
+    scratch = [pltpu.VMEM(x.shape, x.dtype) for x in inputs]
+    scratch += [pltpu.VMEM(weights[n].shape, BF16) for n in order]
     scratch += [
-        pltpu.VMEM((2, pack, heads_half), BF16),
+        pltpu.VMEM((pack, heads_half), BF16),
         pltpu.VMEM((2, pack, heads_half), BF16),
         pltpu.VMEM((rows, heads_half), F32),
         pltpu.VMEM((rows, width), F32),
@@ -332,33 +414,40 @@
         pltpu.VMEM((groups, MEMBERS, pack, half), BF16),
         pltpu.VMEM((groups, 2, pack, half // 2), BF16),
         pltpu.VMEM((groups, 2, pack, half // 2), BF16),
+        dma((len(inputs),)),
         dma((7,)),
         dma((send_count(groups),)),
         dma((5,)),
         dma((groups, MEMBERS, 2)),
         dma((groups, MEMBERS)),
         dma((groups, MEMBERS)),
+        dma((groups, MEMBERS)),
+        dma((groups, MEMBERS)),
         dma((groups,)),
         dma((groups, MEMBERS)),
         dma((groups, 2)),
     ]
-    return pl.pallas_call(
+    attended, block_out = pl.pallas_call(
         functools.partial(kernel, groups),
         out_shape=(
             jax.ShapeDtypeStruct(residual.shape, BF16),
             jax.ShapeDtypeStruct(residual.shape, BF16),
         ),
-        in_specs=[vmem] * 9 + [hbm] * 7,
+        in_specs=[hbm] * 16,
         out_specs=(vmem, vmem),
         scratch_shapes=scratch,
         compiler_params=pltpu.CompilerParams(
             collective_id=0, has_side_effects=True, vmem_limit_bytes=56 * 1024 * 1024
         ),
         name="block",
-    )(
-        queries, fresh_keys, fresh_values, stale_keys, stale_values, residual,
-        norm_gain.reshape(1, width), router.T, expert_ids, *weights,
-    )
+    )(*inputs, *weights)
+    return pl.pallas_call(
+        finish,
+        out_shape=tuple(jax.ShapeDtypeStruct(x.shape, x.dtype) for x in (attended, block_out)),
+        in_specs=[vmem] * 2,
+        out_specs=(vmem, vmem),
+        name="finish",
+    )(attended, block_out)
 
 
 def solution(mesh):

time: 55 us -> 48.1 us (0.87)
  local copies, waits for them, and re-layouts: 5.45 us -> 0 us
  Pallas kernels: 48.6 us -> 47.3 us
    unnamed x3 -> x0, local copies, waits for them, and re-layouts: 4.14 us -> none
    pallas_call x1, Pallas kernels: 48.6 us -> 45.9 us  [per_device(): pl.pallas_call(functools.partial(kernel, groups), out_shape=(jax.ShapeDty...]
    pallas_call x0 -> x1, Pallas kernels: none -> 1.43 us  [per_device(): pl.pallas_call(finish, out_shape=tuple((jax.ShapeDtypeStruct(x.shape, x.d...]
    reshape x1 -> x0, local copies, waits for them, and re-layouts: 1.31 us -> none  [per_device(): norm_gain.reshape(1, width)]
where the time goes in v2:
time: 48.1 us; the launch traced here: 47.9 us
  Pallas kernels  47.3 us (98%)
  between operations  0.64 us (1%)
    pallas_call x1, Pallas kernels, per_device(): pl.pallas_call(functools.partial(kernel, groups), out_shape=(jax.ShapeDty...  45.9 us
    pallas_call x1, Pallas kernels, per_device(): pl.pallas_call(finish, out_shape=tuple((jax.ShapeDtypeStruct(x.shape, x.d...  1.43 us

profile of v2, /device:TPU:0, one launch (start us, length us, event | category | flops | bytes accessed | tf_op | source)
XLA Modules:
  0.0 47.9 jit_solution(5838762381709585657)
XLA Ops:
  0.6 45.9 %block.1 = (bf16[1,8,2560]{2,1,0:T(8,128)(2,1)}, bf16[1,8,2560]{2,1,0:T(8,128)(2,1)}) custom-call(bf16[1,8,1280]{2,1,0:T(8,128)(2,1)} %q_hbm.1, bf16[1,8,1280]{2,1,0:T(8,128)(2,1)} %fk_hbm.1, bf16[1,8,1280]{2,1,0:T(8,128)(2,1)} %fv_hbm.1, bf16[1,8,1280]{2,1,0:T(8,128)(2,1)} %sk_hbm.1, bf16[1,8,1280]{2,1,0:T(8,128)(2,1)} %sv_hbm.1, ...), custom_call_target="tpu_custom_call" | custom-call | tf_op jit(solution)/shard_map/block/pallas_call | solution.py:430
  46.5 1.4 %finish.1 = (bf16[1,8,2560]{2,1,0:T(8,128)(2,1)}, bf16[1,8,2560]{2,1,0:T(8,128)(2,1)}) custom-call(bf16[1,8,2560]{2,1,0:T(8,128)(2,1)} %get-tuple-element.4.attended, bf16[1,8,2560]{2,1,0:T(8,128)(2,1)} %get-tuple-element.5.block_out), custom_call_target="tpu_custom_call" | custom-call | tf_op jit(solution)/shard_map/finish/pallas_call | solution.py:444

commit v3 on v2

--- a/solution.py
+++ b/solution.py
@@ -146,7 +146,7 @@
 
     pl.semaphore_wait(barrier, len(greeted))
 
-    cut = heads_half - heads_half // 5
+    cut = heads_half - 2 * (heads_half // 5)
     for d in steps[1:]:
         send(stale_own, kv.at[groups - d, 0, 0], kv_sem.at[groups - d, 0, 0], at(d, 0, core))
         send(sib_kv.at[0], kv.at[groups - d, 0, 1], kv_sem.at[groups - d, 0, 1], at(d, 0, other))
@@ -246,7 +246,7 @@
     sh_s[...] = stack_halves(other_rows(shared))
     send(sh_s, sh_r, sib_sem.at[4], sibling)
 
-    tok_cut = half - half // 5
+    tok_cut = half - 3 * (half // 10)
 
     def tok_part(d, k):
         return tok.at[d, k, core, :, pl.ds(0, tok_cut)]

time: 48.1 us -> 47.1 us (0.979)
  Pallas kernels: 47.3 us -> 46.3 us
    pallas_call x1, Pallas kernels: 45.9 us -> 44.9 us  [per_device(): pl.pallas_call(functools.partial(kernel, groups), out_shape=(jax.ShapeDty...]
where the time goes in v3:
time: 47.1 us; the launch traced here: 46.9 us
  Pallas kernels  46.3 us (98%)
  between operations  0.64 us (1%)
    pallas_call x1, Pallas kernels, per_device(): pl.pallas_call(functools.partial(kernel, groups), out_shape=(jax.ShapeDty...  44.9 us
    pallas_call x1, Pallas kernels, per_device(): pl.pallas_call(finish, out_shape=tuple((jax.ShapeDtypeStruct(x.shape, x.d...  1.43 us

profile of v3, /device:TPU:0, one launch (start us, length us, event | category | flops | bytes accessed | tf_op | source)
XLA Modules:
  0.0 46.9 jit_solution(10599890588883143970)
XLA Ops:
  0.6 44.9 %block.1 = (bf16[1,8,2560]{2,1,0:T(8,128)(2,1)}, bf16[1,8,2560]{2,1,0:T(8,128)(2,1)}) custom-call(bf16[1,8,1280]{2,1,0:T(8,128)(2,1)} %q_hbm.1, bf16[1,8,1280]{2,1,0:T(8,128)(2,1)} %fk_hbm.1, bf16[1,8,1280]{2,1,0:T(8,128)(2,1)} %fv_hbm.1, bf16[1,8,1280]{2,1,0:T(8,128)(2,1)} %sk_hbm.1, bf16[1,8,1280]{2,1,0:T(8,128)(2,1)} %sv_hbm.1, ...), custom_call_target="tpu_custom_call" | custom-call | tf_op jit(solution)/shard_map/block/pallas_call | solution.py:430
  45.5 1.4 %finish.1 = (bf16[1,8,2560]{2,1,0:T(8,128)(2,1)}, bf16[1,8,2560]{2,1,0:T(8,128)(2,1)}) custom-call(bf16[1,8,2560]{2,1,0:T(8,128)(2,1)} %get-tuple-element.4.attended, bf16[1,8,2560]{2,1,0:T(8,128)(2,1)} %get-tuple-element.5.block_out), custom_call_target="tpu_custom_call" | custom-call | tf_op jit(solution)/shard_map/finish/pallas_call | solution.py:444
